TPU v7x, 128 devices: a whole 4x4x4 slice. The times are simulated.
128 devices in a mesh: dp: 4 (over z), tensor: 32 (over x, y, core).
Axes of the slice: x: 4, y: 4, z: 4, core: 2. Of those that a mesh axis runs over, the one named last changes fastest.
Arguments:
- grads: bfloat16 [4, 2, 8192, 8192], P('dp', None, 'tensor'), may hold values from -60 to 60, as said below
- error: bfloat16 [4, 2, 8192, 8192], P('dp', None, 'tensor'), may hold values from -3 to 3
- q_init: float32 [2, 8192, 32], P(None, 'tensor'), may hold values from -6 to 6
Outputs:
- new_error: bfloat16 [4, 2, 8192, 8192], P('dp', None, 'tensor')
- p_factor: float32 [2, 8192, 32], P(None, 'tensor')
- q_factor: float32 [2, 8192, 32], P(None, 'tensor')
Inputs may be any that keep to these rules, and one draw needn't show every extreme that they name: `grads`: entries of order one, rows of different scales.
All inputs are finite; a program needn't handle non-finite values.
Results may differ from a plain program's by a relative error of at most 0.018.
Values may be sent and summed in bfloat16 or wider, within the bound.
A program may use at most 128 MiB of HBM per device.

v0:
```python
import math

import jax
import jax.numpy as jnp
from jax import lax
from jax.sharding import PartitionSpec as P

ROWS = 8192
ITERS = 2


def by_cholesky(left):
    gram_part = jnp.einsum("mrk,mrj->mkj", left, left, precision=lax.Precision.HIGHEST)
    gram_sum = lax.psum(gram_part, "tensor")
    cholesky_factor = jnp.linalg.cholesky(gram_sum)

    def solve_one(factor, block):
        return jax.scipy.linalg.solve_triangular(factor, block.T, lower=True).T

    return jax.vmap(solve_one)(cholesky_factor, left)


def local(grads, error, q_init):
    merged = (grads[0].astype(jnp.float32) + error[0].astype(jnp.float32)).astype(jnp.bfloat16)
    shrink_by = 1.0 / lax.axis_size("dp")
    share_width = q_init.shape[1]
    right = lax.all_gather(q_init.astype(jnp.bfloat16), "tensor", axis=1, tiled=True)
    basis = None
    for sweep in range(ITERS):
        left = jnp.einsum(
            "mrc,mck->mrk", merged, right.astype(jnp.bfloat16), preferred_element_type=jnp.float32
        )
        left = lax.psum(left.astype(jnp.bfloat16), "dp").astype(jnp.float32) * shrink_by
        basis = by_cholesky(left)
        right_part = jnp.einsum(
            "mrc,mrk->mck", merged, basis.astype(jnp.bfloat16), preferred_element_type=jnp.float32
        )
        right = lax.psum(right_part, ("dp", "tensor")) * shrink_by
    low_rank = jnp.einsum("mrk,mck->mrc", basis, right, precision=lax.Precision.HIGHEST)
    new_error = (merged.astype(jnp.float32) - low_rank).astype(jnp.bfloat16)[None]
    q_factor = lax.dynamic_slice_in_dim(
        right, lax.axis_index("tensor") * share_width, share_width, 1
    )
    return (new_error, basis * math.sqrt(ROWS), q_factor)


def solution(mesh):
    in_specs = (
        P("dp", None, "tensor", None),
        P("dp", None, "tensor", None),
        P(None, "tensor", None),
    )
    out_specs = (P("dp", None, "tensor", None), P(None, "tensor", None), P(None, "tensor", None))
    return jax.shard_map(local, mesh=mesh, in_specs=in_specs, out_specs=out_specs, check_vma=False)
```

profile of v0, /device:TPU:1, one launch (start us, length us, event | category | flops | bytes accessed | tf_op | source)
XLA Modules:
  0.0 703.1 jit_solution(8921783854162598354)
XLA Ops:
  7.2 1.5 convert_element_type.51
  8.8 9.5 %fusion.1 = bf16[2,256,8192]{2,1,0:T(8,128)(2,1)} fusion(bf16[1,2,256,8192]{3,2,1,0:T(8,128)(2,1)} %param.7, bf16[1,2,256,8192]{3,2,1,0:T(8,128)(2,1)} %param.6), kind=kLoop, calls=%fused_computation.3 | loop fusion | flops 16777216 | bytes 25165824 | tf_op jit(solution)/shard_map/convert_element_type | solution.py:24
  18.3 39.0 %all-gather.2.cloned.1.call-done = bf16[2,8192,32]{1,2,0:T(8,128)(2,1)} async-done(((bf16[2,256,32]{1,2,0:T(8,128)(2,1)}), bf16[2,8192,32]{1,2,0:T(8,128)(2,1)}) %all-gather.2.cloned.1.call-update) | async-done | bytes 1048592 | tf_op jit(solution)/shard_map/all_gather | solution.py:27
  57.3 6.2 convolution_convert_fusion.2
  63.5 13.5 %psum.42 = bf16[2,256,32]{1,2,0:T(8,128)(2,1)S(1)} all-reduce(bf16[2,256,32]{1,2,0:T(8,128)(2,1)S(1)} %convolution_convert_fusion.2), channel_id=1, replica_groups=mesh['dp'=4,'tensor'=32] {'dp'}, use_global_device_ids=true, to_apply=%region_0.0 | all-reduce | flops 16384 | bytes 65536 | tf_op jit(solution)/shard_map/psum | solution.py:33
  77.0 0.2 fusion.7
  77.2 122.1 %psum.43 = f32[2,32,32]{1,2,0:T(8,128)S(1)} all-reduce(f32[2,32,32]{1,2,0:T(8,128)S(1)} %fusion.7), channel_id=1, replica_groups=mesh['dp'=4,'tensor'=32] {'tensor'}, use_global_device_ids=true, to_apply=%region_1.0 | all-reduce | flops 2048 | bytes 16384 | tf_op jit(solution)/shard_map/psum | solution.py:14
  199.4 5.9 custom-call.8
  205.5 4.9 custom-call.9
  210.4 0.3 convolution_convert_fusion.1
  210.7 6.2 fusion.23
  217.0 150.2 %all-reduce.3.cloned.1.call-done = f32[2,8192,32]{1,2,0:T(8,128)} async-done(((f32[2,8192,32]{1,2,0:T(8,128)}), f32[2,8192,32]{1,2,0:T(8,128)}) %all-reduce.3.cloned.1.call-update) | async-done | bytes 2097168 | tf_op jit(solution)/shard_map/psum | solution.py:38
  367.2 6.6 convolution_convert_fusion
  373.8 13.3 %psum.45 = bf16[2,256,32]{1,2,0:T(8,128)(2,1)S(1)} all-reduce(bf16[2,256,32]{1,2,0:T(8,128)(2,1)S(1)} %convolution_convert_fusion), channel_id=1, replica_groups=mesh['dp'=4,'tensor'=32] {'dp'}, use_global_device_ids=true, to_apply=%region_5.0 | all-reduce | flops 16384 | bytes 65536 | tf_op jit(solution)/shard_map/psum | solution.py:33
  387.3 121.3 %psum.46 = f32[2,32,32]{1,2,0:T(8,128)S(1)} all-reduce(f32[2,32,32]{1,2,0:T(8,128)S(1)} %fusion.6), channel_id=1, replica_groups=mesh['dp'=4,'tensor'=32] {'tensor'}, use_global_device_ids=true, to_apply=%region_6.9 | all-reduce | flops 2048 | bytes 16384 | tf_op jit(solution)/shard_map/psum | solution.py:14
  508.7 5.9 custom-call.10
  514.8 4.9 custom-call.11
  519.7 0.3 fusion.3
  520.0 6.2 fusion.12
  526.3 0.6 multiply_bitcast_fusion
  526.9 149.6 %all-reduce.5.cloned.1.call-done = f32[2,8192,32]{1,2,0:T(8,128)} async-done(((f32[2,8192,32]{1,2,0:T(8,128)}), f32[2,8192,32]{1,2,0:T(8,128)}) %all-reduce.5.cloned.1.call-update) | async-done | bytes 2097168 | tf_op jit(solution)/shard_map/psum | solution.py:38
  676.5 1.8 broadcast_multiply_fusion
  678.3 0.6 constant_dynamic-slice_fusion
  678.9 17.6 %fusion = bf16[1,2,256,8192]{3,2,1,0:T(8,128)(2,1)} fusion(f32[2,32,256]{2,1,0:T(8,128)S(1)} %fusion.3, bf16[2,256,8192]{2,1,0:T(8,128)(2,1)} %fusion.1, f32[2,8192,32]{1,2,0:T(8,128)} %all-reduce.5.cloned.1.call-done), kind=kOutput, calls=%fused_computation.2 | convolution fusion | flops 1623719936 | bytes 18939904 | tf_op jit(solution)/shard_map/mrk,mck->mrc/dot_general | solution.py:39
  (19 shorter events, 1.0 us)
Async XLA Ops:
  7.2 50.1 %all-gather.2.cloned.1.call-start = ((), (), s32[]{:S(2)}) async-start(), calls=%async_computation | async-start | bytes 1081344 | tf_op jit(solution)/shard_map/all_gather | solution.py:27
  8.7 358.5 %all-reduce.3.cloned.1.call-start = ((), (), s32[]{:S(2)}) async-start(), calls=%async_computation.1 | async-start | bytes 4194304 | tf_op jit(solution)/shard_map/psum | solution.py:38
  217.0 459.5 %all-reduce.5.cloned.1.call-start = ((), (), s32[]{:S(2)}) async-start(), calls=%async_computation.2 | async-start | bytes 4194304 | tf_op jit(solution)/shard_map/psum | solution.py:38
Sparse Core Ops, SparseCore 0:
  10.8 46.4 all-gather.1
  217.1 150.0 all-reduce.2
  526.4 150.0 all-reduce.4
where the time goes:
time: 703 us
  waiting for transfers between devices  339 us (48%)
  blocking collectives  270 us (38%)
  matrix products  43.8 us (6%)
  other arithmetic  35.4 us (5%)
  between operations  13.8 us (2%)
    psum x2, waiting for transfers between devices, local(): right = lax.psum(right_part, ('dp', 'tensor')) * shrink_by  300 us
    psum x2, blocking collectives, by_cholesky(): gram_sum = lax.psum(gram_part, 'tensor')  243 us
    all_gather x1, waiting for transfers between devices, local(): lax.all_gather(q_init.astype(jnp.bfloat16), 'tensor', axis=1, tiled=True)  39 us
    psum x2, blocking collectives, local(): lax.psum(left.astype(jnp.bfloat16), 'dp').astype(jnp.float32) * shrink_by  26.8 us
    dot_general x1, matrix products, local(): jnp.einsum('mrk,mck->mrc', basis, right, precision=lax.Precision.HIGHEST)  17.6 us
  transfers between devices with their start and end apart: 3, of which 3 were waited for; matrix products, arithmetic and copies ran while one was open for 1% of the time, Pallas kernels for 0%

commit v1 on v0

v1 whole, which is shorter than its diff:
```python
import functools
import math

import jax
import jax.numpy as jnp
from jax import lax
from jax.experimental import pallas as pl
from jax.experimental.pallas import tpu as pltpu
from jax.sharding import PartitionSpec as P

ITERS = 2
BF = jnp.bfloat16
F32 = jnp.float32
MESH = pl.DeviceIdType.MESH
HIGHEST = lax.Precision.HIGHEST
RING = (2, 1, 3, 0)
FAR_FIRST = tuple(
    sorted(
        ((dx, dy) for dx in range(4) for dy in range(4) if dx or dy),
        key=lambda s: -(min(s[0], 4 - s[0]) + min(s[1], 4 - s[1])),
    )
)
NEAR_FIRST = FAR_FIRST[::-1]
LOADS = 4


def nt(a, b, **kw):
    return lax.dot_general(a, b, (((1,), (1,)), ((), ())), preferred_element_type=F32, **kw)


def nn(a, b, **kw):
    return lax.dot_general(a, b, (((1,), (0,)), ((), ())), preferred_element_type=F32, **kw)


def inverse_factor(gram):
    n = gram.shape[0]
    row = lax.broadcasted_iota(jnp.int32, (n, 4 * n), 0)
    lane = lax.broadcasted_iota(jnp.int32, (n, 4 * n), 1)
    work = jnp.where(lane == row + n, 1.0, gram)
    for j in range(n):
        column = jnp.broadcast_to(work[:, j : j + 1], work.shape)
        pivot = jnp.broadcast_to(column[j : j + 1, :], work.shape)
        line = jnp.broadcast_to(work[j : j + 1, :], work.shape)
        work = work - jnp.where(row > j, column / pivot, 0.0) * line
    diagonal = jnp.sum(jnp.where(lane == row, work, 0.0), axis=1, keepdims=True)
    work = work * lax.rsqrt(diagonal)
    return work[:, n : 2 * n]


def factors_kernel(
    grads, error, q_init, merged, right_out, basis_out,
    error_vm, q_vm, right_in, left_part, left_sum, left_bf, part, part_in, chip_sum, plane_in,
    z_in, gram_own, gram_core, gram_in, inv_own, q_stage,
    load_sem, q_load_sem, q_core_sem, ag_send, ag_recv, fwd_send, fwd_recv,
    left_send, left_recv, core_send, core_recv, rs_send, rs_recv, z_send, z_recv,
    gc_sem, g_send, g_recv, inv_sem,
):
    z = lax.axis_index("dp")
    t = lax.axis_index("tensor")
    core = lax.rem(t, 2)
    other = 1 - core
    chip = t // 2
    x, y = chip // 4, lax.rem(chip, 4)

    def chip_at(dx, dy):
        return lax.rem(x + dx, 4) * 4 + lax.rem(y + dy, 4)

    def plane(dx, dy):
        return (z, chip_at(dx, dy) * 2 + core)

    def depth(dz):
        return (lax.rem(z + dz, 4), t)

    sibling = (z, chip * 2 + other)
    started = []

    def send(src, dst, send_sem, recv_sem, device):
        copy = pltpu.make_async_remote_copy(
            src_ref=src, dst_ref=dst, send_sem=send_sem, recv_sem=recv_sem, device_id=device, device_id_type=MESH
        )
        copy.start()
        started.append(copy)
        return copy

    def landed(ref, sem):
        pltpu.make_async_copy(ref, ref, sem).wait()

    q_load = pltpu.make_async_copy(q_init, q_vm, q_load_sem)
    q_load.start()
    loads = []
    size = 256 // LOADS
    for m in range(2):
        for i in range(LOADS):
            rows = pl.ds(i * size, size)
            k = (m * LOADS + i) * 2
            pair = (
                pltpu.make_async_copy(grads.at[0, m, rows], merged.at[m, rows], load_sem.at[k]),
                pltpu.make_async_copy(error.at[0, m, rows], error_vm.at[m, rows], load_sem.at[k + 1]),
            )
            for copy in pair:
                copy.start()
            loads.append((m, rows, pair))

    barrier = pltpu.get_barrier_semaphore()
    peers = [plane(dx, dy) for dx, dy in FAR_FIRST] + [depth(dz) for dz in (2, 1, 3)] + [sibling]
    for peer in peers:
        pl.semaphore_signal(barrier, inc=1, device_id=peer, device_id_type=MESH)

    q_load.wait()
    half = pl.ds(pl.multiple_of(core * 256, 256), 256)
    right_in[0, core, chip, :, half] = q_vm[core].astype(BF)
    q_stage[...] = q_vm[other].astype(BF)
    pl.semaphore_wait(barrier, len(peers))
    send(q_stage, right_in.at[0, other, chip, :, half], q_core_sem.at[0], q_core_sem.at[1], sibling)

    def rights(stage):
        return right_in.at[stage] if stage < 2 else right_out

    def gather(stage, use):
        right = rights(stage)
        block = right.at[core, chip]
        for k, (dx, dy) in enumerate(FAR_FIRST):
            send(block, block, ag_send.at[stage, k], ag_recv.at[stage, k], plane(dx, dy))
        send(block, block, fwd_send.at[stage, 15], fwd_recv.at[stage, 15], sibling)
        use(core, chip)
        behind = [(15, chip)]

        def take():
            k, p = behind.pop(0)
            landed(right.at[other, p], fwd_recv.at[stage, k])
            use(other, p)

        for dx, dy in NEAR_FIRST:
            k = FAR_FIRST.index((dx, dy))
            p = chip_at(4 - dx, 4 - dy)
            block = right.at[core, p]
            landed(block, ag_recv.at[stage, k])
            send(block, block, fwd_send.at[stage, k], fwd_recv.at[stage, k], sibling)
            use(core, p)
            behind.append((k, p))
            if len(behind) > 2:
                take()
        while behind:
            take()

    for m, rows, pair in loads:
        for copy in pair:
            copy.wait()
        merged[m, rows] = (merged[m, rows].astype(F32) + error_vm[m, rows].astype(F32)).astype(BF)

    got = right_in.at[0, core, chip, :, pl.ds(pl.multiple_of(other * 256, 256), 256)]
    landed(got, q_core_sem.at[1])

    for sweep in range(ITERS):
        acc = {True: jnp.zeros((32, 256), F32), False: jnp.zeros((32, 256), F32)}
        right = rights(sweep)

        def add_left(m, p):
            cols = pl.ds(pl.multiple_of(p * 512, 512), 512)
            acc[m is core] += nt(right[m, p], merged[m, :, cols])

        gather(sweep, add_left)
        left_part[sweep, z, core] = acc[True].astype(BF)
        left_part[sweep, z, other] = acc[False].astype(BF)

        own = left_part.at[sweep, z]
        for k, dz in enumerate((2, 1, 3)):
            send(own, own, left_send.at[sweep, k], left_recv.at[sweep], depth(dz))
        landed(left_part.at[sweep, pl.ds(0, 3)], left_recv.at[sweep])
        for m in range(2):
            total = left_part[sweep, 0, m].astype(F32)
            for k in range(1, 4):
                total += left_part[sweep, k, m].astype(F32)
            left_sum[m] = total
            left_bf[m] = total.astype(BF)

        for m in range(2):
            gram_own[sweep, m, :, 0:32] = nt(left_sum[m], left_sum[m], precision=HIGHEST)
            gram_own[sweep, m, :, 32:128] = jnp.zeros((32, 96), F32)
        send(gram_own.at[sweep, other], gram_core.at[sweep], gc_sem.at[sweep, 0], gc_sem.at[sweep, 1], sibling)

        for j, dx in enumerate(RING):
            first = lax.rem(x + dx, 4) * 4
            for i in range(4):
                cols = pl.ds(pl.multiple_of((first + i) * 512, 512), 512)
                part[sweep, first + i] = nn(left_bf[other], merged[other, :, cols]).astype(BF)
            blocks = pl.ds(first, 4)
            send(part.at[sweep, blocks], part_in.at[sweep, blocks], core_send.at[sweep, j], core_recv.at[sweep, j], sibling)
        for j, dx in enumerate(RING):
            first = lax.rem(x + dx, 4) * 4
            partial = []
            for i in range(4):
                cols = pl.ds(pl.multiple_of((first + i) * 512, 512), 512)
                partial.append(nn(left_bf[core], merged[core, :, cols]))
            landed(part_in.at[sweep, pl.ds(first, 4)], core_recv.at[sweep, j])
            for i in range(4):
                chip_sum[sweep, first + i] = (partial[i] + part_in[sweep, first + i].astype(F32)).astype(BF)
            for dy in RING:
                if (dx, dy) != (0, 0):
                    k = FAR_FIRST.index((dx, dy))
                    send(
                        chip_sum.at[sweep, chip_at(dx, dy)], plane_in.at[sweep, chip],
                        rs_send.at[sweep, k], rs_recv.at[sweep], plane(dx, dy),
                    )
            if j == 0:
                landed(gram_core.at[sweep], gc_sem.at[sweep, 1])
                gram = gram_own[sweep, core] + gram_core[sweep]
                packed = gram[0:8]
                for i in range(1, 4):
                    packed += pltpu.roll(gram[i * 8 : i * 8 + 8], 32 * i, 1)
                gram_in[sweep, chip] = packed
                for k, (ex, ey) in enumerate(FAR_FIRST):
                    send(gram_in.at[sweep, chip], gram_in.at[sweep, chip], g_send.at[sweep, k], g_recv.at[sweep], plane(ex, ey))
        plane_in[sweep, chip] = chip_sum[sweep, chip]

        landed(plane_in.at[sweep, pl.ds(0, 15)], rs_recv.at[sweep])
        total = plane_in[sweep, 0].astype(F32)
        for p in range(1, 16):
            total += plane_in[sweep, p].astype(F32)
        z_in[sweep, z] = total.astype(BF)
        own = z_in.at[sweep, z]
        for k, dz in enumerate((2, 1, 3)):
            send(own, own, z_send.at[sweep, k], z_recv.at[sweep], depth(dz))

        landed(gram_in.at[sweep, pl.ds(0, 15)], g_recv.at[sweep])
        packed = gram_in[sweep, 0]
        for p in range(1, 16):
            packed += gram_in[sweep, p]
        lane = lax.broadcasted_iota(jnp.int32, (8, 128), 1)
        lines = [packed] + [pltpu.roll(packed, 128 - 32 * i, 1) for i in range(1, 4)]
        gram = jnp.concatenate([jnp.where(lane < 32, line, 0.0) for line in lines], axis=0)
        inverse = inverse_factor(gram)

        landed(z_in.at[sweep, pl.ds(0, 3)], z_recv.at[sweep])
        total = z_in[sweep, 0].astype(F32)
        for k in range(1, 4):
            total += z_in[sweep, k].astype(F32)
        rights(sweep + 1)[core, chip] = (nn(inverse, total, precision=HIGHEST) * 0.25).astype(BF)

        if sweep == ITERS - 1:
            inv_own[core, :, 0:32] = inverse
            inv_own[core, :, 32:128] = jnp.zeros((32, 96), F32)
            mine = inv_own.at[core]
            send(mine, mine, inv_sem.at[0], inv_sem.at[1], sibling)

    gather(ITERS, lambda m, p: None)
    landed(inv_own.at[other], inv_sem.at[1])
    for m in range(2):
        basis_out[m] = nn(inv_own[m, :, 0:32], left_sum[m], precision=HIGHEST)
    for copy in started:
        copy.wait_send()


def apply_kernel(merged, right, basis, new_error, p_factor, q_factor, out_vm, sem):
    chip = lax.axis_index("tensor") // 2
    core = lax.rem(lax.axis_index("tensor"), 2)
    copies = []
    for m in range(2):
        high = basis[m].astype(BF)
        low = (basis[m] - high.astype(F32)).astype(BF)
        both = jnp.concatenate([high, low], axis=0)
        for p in range(16):
            block = jnp.concatenate([right[m, p], right[m, p]], axis=0)
            cols = pl.ds(p * 512, 512)
            low_rank = lax.dot_general(both, block, (((0,), (0,)), ((), ())), preferred_element_type=F32)
            out_vm[m, :, cols] = (merged[m, :, cols].astype(F32) - low_rank).astype(BF)
            if p % 4 == 3:
                cols = pl.ds((p - 3) * 512, 2048)
                copy = pltpu.make_async_copy(out_vm.at[m, :, cols], new_error.at[0, m, :, cols], sem.at[m * 4 + p // 4])
                copy.start()
                copies.append(copy)
        p_factor[m] = basis[m] * math.sqrt(8192)
        q_factor[m] = right[m, chip, :, pl.ds(pl.multiple_of(core * 256, 256), 256)].astype(F32)
    for copy in copies:
        copy.wait()


def local(grads, error, q_init):
    hbm = pl.BlockSpec(memory_space=pltpu.HBM)
    vmem = pl.BlockSpec(memory_space=pltpu.VMEM)
    dma = pltpu.SemaphoreType.DMA
    merged, right, basis = pl.pallas_call(
        factors_kernel,
        name="factors",
        out_shape=(
            pltpu.VMEM((2, 256, 8192), BF),
            pltpu.VMEM((2, 16, 32, 512), BF),
            pltpu.VMEM((2, 32, 256), F32),
        ),
        in_specs=[hbm] * 3,
        out_specs=(vmem,) * 3,
        scratch_shapes=[
            pltpu.VMEM((2, 256, 8192), BF),
            pltpu.VMEM((2, 32, 256), F32),
            pltpu.VMEM((2, 2, 16, 32, 512), BF),
            pltpu.VMEM((2, 4, 2, 32, 256), BF),
            pltpu.VMEM((2, 32, 256), F32),
            pltpu.VMEM((2, 32, 256), BF),
            pltpu.VMEM((2, 16, 32, 512), BF),
            pltpu.VMEM((2, 16, 32, 512), BF),
            pltpu.VMEM((2, 16, 32, 512), BF),
            pltpu.VMEM((2, 16, 32, 512), BF),
            pltpu.VMEM((2, 4, 32, 512), BF),
            pltpu.VMEM((2, 2, 32, 128), F32),
            pltpu.VMEM((2, 32, 128), F32),
            pltpu.VMEM((2, 16, 8, 128), F32),
            pltpu.VMEM((2, 32, 128), F32),
            pltpu.VMEM((32, 256), BF),
            dma((4 * LOADS,)), dma, dma((2,)),
            dma((3, 15)), dma((3, 15)), dma((3, 16)), dma((3, 16)),
            dma((2, 3)), dma((2,)), dma((2, 4)), dma((2, 4)), dma((2, 15)), dma((2,)), dma((2, 3)), dma((2,)),
            dma((2, 2)), dma((2, 15)), dma((2,)), dma((2,)),
        ],
        compiler_params=pltpu.CompilerParams(
            collective_id=0, has_side_effects=True, vmem_limit_bytes=32 << 20
        ),
    )(
        pltpu.with_memory_space_constraint(grads, pltpu.HBM),
        pltpu.with_memory_space_constraint(error, pltpu.HBM),
        q_init.transpose(0, 2, 1),
    )
    new_error, p_factor, q_factor = pl.pallas_call(
        apply_kernel,
        name="apply",
        out_shape=(
            jax.ShapeDtypeStruct((1, 2, 256, 8192), BF),
            jax.ShapeDtypeStruct((2, 32, 256), F32),
            jax.ShapeDtypeStruct((2, 32, 256), F32),
        ),
        in_specs=[vmem] * 3,
        out_specs=(hbm, vmem, vmem),
        scratch_shapes=[pltpu.VMEM((2, 256, 8192), BF), dma((8,))],
        compiler_params=pltpu.CompilerParams(vmem_limit_bytes=24 << 20),
    )(merged, right, basis)
    return new_error, p_factor.transpose(0, 2, 1), q_factor.transpose(0, 2, 1)


def solution(mesh):
    in_specs = (
        P("dp", None, "tensor", None),
        P("dp", None, "tensor", None),
        P(None, "tensor", None),
    )
    out_specs = (P("dp", None, "tensor", None), P(None, "tensor", None), P(None, "tensor", None))
    return jax.shard_map(local, mesh=mesh, in_specs=in_specs, out_specs=out_specs, check_vma=False)
```

time: 703 us -> 101 us (0.14)
  waiting for transfers between devices: 339 us -> 0 us
  blocking collectives: 270 us -> 0 us
  Pallas kernels: 0 us -> 99.8 us
  matrix products: 43.8 us -> 0 us
  other arithmetic: 35.4 us -> 0 us
  between operations: 13.8 us -> 0.65 us
    psum x2 -> x0, waiting for transfers between devices: 300 us -> none  [local(): right = lax.psum(right_part, ('dp', 'tensor')) * shrink_by]
    psum x4 -> x0, blocking collectives: 270 us -> none  [the longest x2 243 us: by_cholesky(): gram_sum = lax.psum(gram_part, 'tensor')]
    pallas_call x0 -> x2, Pallas kernels: none -> 99.8 us  [the longest x1 95.3 us: local(): pl.pallas_call(factors_kernel, name='factors', out_shape=(pltpu.VMEM((2,...]
    dot_general x7 -> x0, matrix products: 43.2 us -> none  [the longest x1 17.6 us: local(): jnp.einsum('mrk,mck->mrc', basis, right, precision=lax.Precision.HIGHEST)]
    all_gather x1 -> x0, waiting for transfers between devices: 39 us -> none  [local(): lax.all_gather(q_init.astype(jnp.bfloat16), 'tensor', axis=1, tiled=True)]
    another operation x12 -> x0, other arithmetic: 22 us -> none  [the longest x7 12 us: by_cholesky(): cholesky_factor = jnp.linalg.cholesky(gram_sum)]
    convert_element_type x2 -> x0, other arithmetic: 10.9 us -> none  [the longest x1 9.48 us: local(): (grads[0].astype(jnp.float32) + error[0].astype(jnp.float32)).astype(jnp....]
  transfers between devices with their start and end apart: 3 -> 0, of which waited for: 3 -> 0; matrix products, arithmetic and copies ran while one was open for 1% -> 0% of each run, Pallas kernels for 0% -> 0%
where the time goes in v1:
time: 101 us
  Pallas kernels  99.8 us (99%)
    pallas_call x1, Pallas kernels, local(): pl.pallas_call(factors_kernel, name='factors', out_shape=(pltpu.VMEM((2,...  95.3 us
    pallas_call x1, Pallas kernels, local(): pl.pallas_call(apply_kernel, name='apply', out_shape=(jax.ShapeDtypeStruc...  4.48 us

profile of v1, /device:TPU:1, one launch (start us, length us, event | category | flops | bytes accessed | tf_op | source)
XLA Modules:
  0.0 101.3 jit_solution(2932074472120913193)
XLA Ops:
  0.6 0.0 copy-start
  0.6 0.8 copy-done
  1.5 95.3 %factors.1 = (bf16[2,256,8192]{2,1,0:T(8,128)(2,1)S(1)}, bf16[2,16,32,512]{3,2,1,0:T(8,128)(2,1)S(1)}, f32[2,32,256]{2,1,0:T(8,128)S(1)}) custom-call(bf16[1,2,256,8192]{3,2,1,0:T(8,128)(2,1)} %grads.1, bf16[1,2,256,8192]{3,2,1,0:T(8,128)(2,1)} %error.1, f32[2,32,256]{2,1,0:T(8,128)S(1)} %bitcast.3), custom_call_target="tpu_custom_call" | custom-call | tf_op jit(solution)/shard_map/factors/pallas_call | solution.py:282
  96.8 4.5 %apply.1 = (bf16[1,2,256,8192]{3,2,1,0:T(8,128)(2,1)}, f32[2,32,256]{2,1,0:T(8,128)}, f32[2,32,256]{2,1,0:T(8,128)}) custom-call(bf16[2,256,8192]{2,1,0:T(8,128)(2,1)S(1)} %get-tuple-element.9.merged, bf16[2,16,32,512]{3,2,1,0:T(8,128)(2,1)S(1)} %get-tuple-element.10.right, f32[2,32,256]{2,1,0:T(8,128)S(1)} %get-tuple-element.11.basis), custom_call_target="tpu_custom_call" | custom-call | tf_op jit(solution)/shard_map/apply/pallas_call | solution.py:322
Async XLA Ops:
  0.6 0.8 copy-start

commit v2 on v0

v2 whole, which is shorter than its diff:
```python
import math

import jax
import jax.numpy as jnp
from jax import lax
from jax.experimental import pallas as pl
from jax.experimental.pallas import tpu as pltpu
from jax.sharding import PartitionSpec as P

ITERS = 2
BF = jnp.bfloat16
F32 = jnp.float32
MESH = pl.DeviceIdType.MESH
HIGHEST = lax.Precision.HIGHEST
FAR_FIRST = tuple(
    sorted(
        ((dx, dy) for dx in range(4) for dy in range(4) if dx or dy),
        key=lambda s: -(min(s[0], 4 - s[0]) + min(s[1], 4 - s[1])),
    )
)
NEAR_FIRST = FAR_FIRST[::-1]
LOADS = 4
PANEL = 16


def nt(a, b, **kw):
    return lax.dot_general(a, b, (((1,), (1,)), ((), ())), preferred_element_type=F32, **kw)


def nn(a, b, **kw):
    return lax.dot_general(a, b, (((1,), (0,)), ((), ())), preferred_element_type=F32, **kw)


def inverse_factor(gram):
    n = gram.shape[0]
    row = lax.broadcasted_iota(jnp.int32, (n, 4 * n), 0)
    lane = lax.broadcasted_iota(jnp.int32, (n, 4 * n), 1)
    work = jnp.where(lane == row + n, 1.0, gram)
    for first in range(0, n, PANEL):
        spread = [jnp.broadcast_to(work[:, first + i : first + i + 1], work.shape) for i in range(PANEL)]
        for i in range(PANEL):
            j = first + i
            share = jnp.where(row > j, spread[i] * (1.0 / spread[i][j : j + 1, :]), 0.0)
            for k in range(i + 1, PANEL):
                spread[k] = spread[k] - share * spread[k][j : j + 1, :]
            work = work - share * work[j : j + 1, :]
    diagonal = jnp.sum(jnp.where(lane == row, work, 0.0), axis=1, keepdims=True)
    work = work * lax.rsqrt(diagonal)
    return work[:, n : 2 * n]


def factors_kernel(
    grads, error, q_init, rest, p_out, q_out,
    merged, sibling_rows, q_vm, q_stage, right_in, right_last, left_part, left_sum, left_bf,
    chip_sum, plane_in, z_in, gram_pad, gram_in, basis, basis_stage, basis_t,
    load_sem, q_load_sem, q_core_sem, swap_send, swap_recv, ag_send, ag_recv, fwd_send, fwd_recv,
    left_send, left_recv, rs_send, rs_recv, z_send, z_recv, g_send, g_recv, basis_sem,
):
    z = lax.axis_index("dp")
    t = lax.axis_index("tensor")
    core = lax.rem(t, 2)
    other = 1 - core
    chip = t // 2
    x, y = chip // 4, lax.rem(chip, 4)

    def chip_at(dx, dy):
        return lax.rem(x + dx, 4) * 4 + lax.rem(y + dy, 4)

    def plane(dx, dy):
        return (z, chip_at(dx, dy) * 2 + core)

    def depth(dz):
        return (lax.rem(z + dz, 4), t)

    sibling = (z, chip * 2 + other)
    started = []

    def send(src, dst, send_sem, recv_sem, device):
        copy = pltpu.make_async_remote_copy(
            src_ref=src, dst_ref=dst, send_sem=send_sem, recv_sem=recv_sem, device_id=device, device_id_type=MESH
        )
        copy.start()
        started.append(copy)

    def landed(ref, sem):
        pltpu.make_async_copy(ref, ref, sem).wait()

    def columns(p, h):
        return pl.ds(pl.multiple_of(p * 512 + h * 256, 256), 256)

    q_load = pltpu.make_async_copy(q_init, q_vm, q_load_sem)
    q_load.start()
    loads = []
    size = 256 // LOADS
    for m in range(2):
        for i in range(LOADS):
            which = (other, core)[m]
            rows = pl.ds(i * size, size)
            k = (m * LOADS + i) * 2
            pair = (
                pltpu.make_async_copy(grads.at[0, which, rows], merged.at[which, rows], load_sem.at[k]),
                pltpu.make_async_copy(error.at[0, which, rows], rest.at[which, rows], load_sem.at[k + 1]),
            )
            for copy in pair:
                copy.start()
            loads.append((which, rows, pair))

    barrier = pltpu.get_barrier_semaphore()
    peers = [plane(dx, dy) for dx, dy in FAR_FIRST] + [depth(dz) for dz in (2, 1, 3)] + [sibling]
    for peer in peers:
        pl.semaphore_signal(barrier, inc=1, device_id=peer, device_id_type=MESH)

    def merge(which, rows, pair):
        for copy in pair:
            copy.wait()
        merged[which, rows] = (merged[which, rows].astype(F32) + rest[which, rows].astype(F32)).astype(BF)

    def gather(stage, h, right):
        for k, (dx, dy) in enumerate(FAR_FIRST):
            send(right.at[h, chip], right.at[h, chip], ag_send.at[stage, h, k], ag_recv.at[stage, h, k], plane(dx, dy))

    def arrivals(stage, h, right):
        yield 15, chip
        for dx, dy in NEAR_FIRST:
            k = FAR_FIRST.index((dx, dy))
            p = chip_at(4 - dx, 4 - dy)
            landed(right.at[h, p], ag_recv.at[stage, h, k])
            yield k, p

    q_load.wait()
    right_in[0, core, chip] = q_vm[core].astype(BF)
    q_stage[...] = q_vm[other].astype(BF)
    for load in loads[:LOADS]:
        merge(*load)
    pl.semaphore_wait(barrier, len(peers))
    send(q_stage, right_in.at[0, core, chip], q_core_sem.at[0], q_core_sem.at[1], sibling)
    gather(0, core, right_in.at[0])
    swaps = []
    for i, (_, rows, _) in enumerate(loads[:LOADS]):
        copy = pltpu.make_async_remote_copy(
            src_ref=merged.at[other, rows], dst_ref=sibling_rows.at[rows], send_sem=swap_send.at[i],
            recv_sem=swap_recv.at[i], device_id=sibling, device_id_type=MESH,
        )
        copy.start()
        swaps.append(copy)
    landed(right_in.at[0, other, chip], q_core_sem.at[1])
    gather(0, other, right_in.at[0])
    for load in loads[LOADS:]:
        merge(*load)

    inverse = None
    for sweep in range(ITERS):
        right = right_in.at[sweep]
        own_rows = jnp.zeros((32, 256), F32)
        its_rows = jnp.zeros((32, 256), F32)
        here = []
        for i, h in enumerate((core, other) if sweep == 0 else (0, 1)):
            if sweep == 0 and i == 1:
                for copy in swaps:
                    copy.wait()
                for early, p in here:
                    its_rows += nt(right[early, p], sibling_rows[:, columns(p, early)])
            for _, p in arrivals(sweep, h, right):
                own_rows += nt(right[h, p], merged[core, :, columns(p, h)])
                if sweep == 0 and i == 0:
                    here.append((h, p))
                else:
                    its_rows += nt(right[h, p], sibling_rows[:, columns(p, h)])
        left_part[sweep, z, core] = own_rows.astype(BF)
        left_part[sweep, z, other] = its_rows.astype(BF)

        own = left_part.at[sweep, z]
        for k, dz in enumerate((2, 1, 3)):
            send(own, own, left_send.at[sweep, k], left_recv.at[sweep], depth(dz))
        landed(left_part.at[sweep, pl.ds(0, 3)], left_recv.at[sweep])
        for i in range(2):
            total = left_part[sweep, 0, i].astype(F32)
            for k in range(1, 4):
                total += left_part[sweep, k, i].astype(F32)
            left_sum[i] = total
            left_bf[i] = total.astype(BF)

        for h in range(2):
            for k, (dx, dy) in enumerate(FAR_FIRST + ((0, 0),)):
                p = chip_at(dx, dy)
                block = nn(left_bf[core], merged[core, :, columns(p, h)])
                block = (block + nn(left_bf[other], sibling_rows[:, columns(p, h)])).astype(BF)
                if k == 15:
                    plane_in[sweep, h, chip] = block
                else:
                    chip_sum[sweep, h, p] = block
                    send(
                        chip_sum.at[sweep, h, p], plane_in.at[sweep, h, chip],
                        rs_send.at[sweep, h, k], rs_recv.at[sweep, h], plane(dx, dy),
                    )
            if h == 0:
                gram_pad[:, 0:32] = nt(left_sum[0], left_sum[0], precision=HIGHEST) + nt(
                    left_sum[1], left_sum[1], precision=HIGHEST
                )
                gram_pad[:, 32:128] = jnp.zeros((32, 96), F32)
                packed = gram_pad[0:8]
                for i in range(1, 4):
                    packed += pltpu.roll(gram_pad[i * 8 : i * 8 + 8], 32 * i, 1)
                gram_in[sweep, chip] = packed
                for k, (dx, dy) in enumerate(FAR_FIRST):
                    send(gram_in.at[sweep, chip], gram_in.at[sweep, chip], g_send.at[sweep, k], g_recv.at[sweep], plane(dx, dy))

        for h in range(2):
            landed(plane_in.at[sweep, h, pl.ds(0, 15)], rs_recv.at[sweep, h])
            total = plane_in[sweep, h, 0].astype(F32)
            for p in range(1, 16):
                total += plane_in[sweep, h, p].astype(F32)
            z_in[sweep, h, z] = total.astype(BF)
            own = z_in.at[sweep, h, z]
            for k, dz in enumerate((2, 1, 3)):
                send(own, own, z_send.at[sweep, h, k], z_recv.at[sweep, h], depth(dz))
            if h == 0:
                landed(gram_in.at[sweep, pl.ds(0, 15)], g_recv.at[sweep])
                packed = gram_in[sweep, 0]
                for p in range(1, 16):
                    packed += gram_in[sweep, p]
                lane = lax.broadcasted_iota(jnp.int32, (8, 128), 1)
                lines = [packed] + [pltpu.roll(packed, 128 - 32 * i, 1) for i in range(1, 4)]
                gram = jnp.concatenate([jnp.where(lane < 32, line, 0.0) for line in lines], axis=0)
                inverse = inverse_factor(gram)
        if sweep == ITERS - 1:
            basis_stage[...] = nn(inverse, left_sum[other], precision=HIGHEST)
            send(basis_stage, basis.at[core], basis_sem.at[0], basis_sem.at[1], sibling)
            basis[core] = nn(inverse, left_sum[core], precision=HIGHEST)
        sent = started[:]
        started.clear()
        after = right_in.at[sweep + 1] if sweep < ITERS - 1 else right_last.at[core]
        for h in range(2):
            landed(z_in.at[sweep, h, pl.ds(0, 3)], z_recv.at[sweep, h])
            total = z_in[sweep, h, 0].astype(F32)
            for k in range(1, 4):
                total += z_in[sweep, h, k].astype(F32)
            after[h, chip] = (nn(inverse, total, precision=HIGHEST) * 0.25).astype(BF)
            gather(sweep + 1, h, after)
        for copy in sent:
            copy.wait_send()

    landed(basis.at[other], basis_sem.at[1])
    factor = []
    for m in range(2):
        p_out[m] = basis[m] * math.sqrt(8192)
        tall = basis[m].T
        high = tall.astype(BF)
        low = (tall - high.astype(F32)).astype(BF)
        factor.append(jnp.concatenate([high, low], axis=1))
    basis_t[0], basis_t[1] = factor

    def subtract(m, h, p):
        block = right_last[m, h, p]
        low_rank = nn(basis_t[m], jnp.concatenate([block, block], axis=0))
        cols = columns(p, h)
        rest[m, :, cols] = (merged[m, :, cols].astype(F32) - low_rank).astype(BF)

    behind = []

    def take():
        group = behind.pop(0)
        for h, k, p in group:
            landed(right_last.at[other, h, p], fwd_recv.at[h, k])
        for h, _, p in group:
            subtract(other, h, p)

    for h in range(2):
        coming = arrivals(ITERS, h, right_last.at[core])
        for _ in range(4):
            group = []
            for _ in range(4):
                k, p = next(coming)
                block = right_last.at[core, h, p]
                send(block, block, fwd_send.at[h, k], fwd_recv.at[h, k], sibling)
                group.append((h, k, p))
            for _, _, p in group:
                subtract(core, h, p)
            behind.append(group)
            if len(behind) > 4:
                take()
    while behind:
        take()
    for m in range(2):
        q_out[m] = right_last[m, core, chip].astype(F32)
    for copy in started:
        copy.wait_send()


def store_kernel(rest, p_in, q_in, new_error, p_factor, q_factor, sem):
    copies = [
        pltpu.make_async_copy(p_in, p_factor, sem.at[16]),
        pltpu.make_async_copy(q_in, q_factor, sem.at[17]),
    ]
    for m in range(2):
        for i in range(8):
            rows = pl.ds(i * 32, 32)
            copies.append(pltpu.make_async_copy(rest.at[m, rows], new_error.at[0, m, rows], sem.at[m * 8 + i]))
    for copy in copies:
        copy.start()
    for copy in copies:
        copy.wait()


def local(grads, error, q_init):
    hbm = pl.BlockSpec(memory_space=pltpu.HBM)
    vmem = pl.BlockSpec(memory_space=pltpu.VMEM)
    dma = pltpu.SemaphoreType.DMA
    rest, p_factor, q_factor = pl.pallas_call(
        factors_kernel,
        name="factors",
        out_shape=(
            pltpu.VMEM((2, 256, 8192), BF),
            pltpu.VMEM((2, 32, 256), F32),
            pltpu.VMEM((2, 32, 256), F32),
        ),
        in_specs=[hbm] * 3,
        out_specs=(vmem,) * 3,
        scratch_shapes=[
            pltpu.VMEM((2, 256, 8192), BF),
            pltpu.VMEM((256, 8192), BF),
            pltpu.VMEM((2, 32, 256), F32),
            pltpu.VMEM((32, 256), BF),
            pltpu.VMEM((2, 2, 16, 32, 256), BF),
            pltpu.VMEM((2, 2, 16, 32, 256), BF),
            pltpu.VMEM((2, 4, 2, 32, 256), BF),
            pltpu.VMEM((2, 32, 256), F32),
            pltpu.VMEM((2, 32, 256), BF),
            pltpu.VMEM((2, 2, 16, 32, 256), BF),
            pltpu.VMEM((2, 2, 16, 32, 256), BF),
            pltpu.VMEM((2, 2, 4, 32, 256), BF),
            pltpu.VMEM((32, 128), F32),
            pltpu.VMEM((2, 16, 8, 128), F32),
            pltpu.VMEM((2, 32, 256), F32),
            pltpu.VMEM((32, 256), F32),
            pltpu.VMEM((2, 256, 64), BF),
            dma((4 * LOADS,)), dma, dma((2,)), dma((LOADS,)), dma((LOADS,)),
            dma((3, 2, 15)), dma((3, 2, 15)), dma((2, 16)), dma((2, 16)),
            dma((2, 3)), dma((2,)), dma((2, 2, 15)), dma((2, 2)), dma((2, 2, 3)), dma((2, 2)),
            dma((2, 15)), dma((2,)), dma((2,)),
        ],
        compiler_params=pltpu.CompilerParams(
            collective_id=0, has_side_effects=True, vmem_limit_bytes=32 << 20
        ),
    )(
        pltpu.with_memory_space_constraint(grads, pltpu.HBM),
        pltpu.with_memory_space_constraint(error, pltpu.HBM),
        pltpu.with_memory_space_constraint(q_init.transpose(0, 2, 1), pltpu.HBM),
    )
    new_error, p_factor, q_factor = pl.pallas_call(
        store_kernel,
        name="store",
        out_shape=(
            pltpu.HBM((1, 2, 256, 8192), BF),
            pltpu.HBM((2, 32, 256), F32),
            pltpu.HBM((2, 32, 256), F32),
        ),
        in_specs=[vmem] * 3,
        out_specs=(hbm,) * 3,
        scratch_shapes=[dma((18,))],
        compiler_params=pltpu.CompilerParams(vmem_limit_bytes=24 << 20),
    )(rest, p_factor, q_factor)
    return new_error, p_factor.transpose(0, 2, 1), q_factor.transpose(0, 2, 1)


def solution(mesh):
    in_specs = (
        P("dp", None, "tensor", None),
        P("dp", None, "tensor", None),
        P(None, "tensor", None),
    )
    out_specs = (P("dp", None, "tensor", None), P(None, "tensor", None), P(None, "tensor", None))
    return jax.shard_map(local, mesh=mesh, in_specs=in_specs, out_specs=out_specs, check_vma=False)
```

time: 703 us -> 79 us (0.11)
  waiting for transfers between devices: 339 us -> 0 us
  blocking collectives: 270 us -> 0 us
  Pallas kernels: 0 us -> 78.1 us
  matrix products: 43.8 us -> 0 us
  other arithmetic: 35.4 us -> 0 us
  between operations: 13.8 us -> 0.8 us
    psum x2 -> x0, waiting for transfers between devices: 300 us -> none  [local(): right = lax.psum(right_part, ('dp', 'tensor')) * shrink_by]
    psum x4 -> x0, blocking collectives: 270 us -> none  [the longest x2 243 us: by_cholesky(): gram_sum = lax.psum(gram_part, 'tensor')]
    pallas_call x0 -> x2, Pallas kernels: none -> 78.1 us  [the longest x1 74.6 us: local(): pl.pallas_call(factors_kernel, name='factors', out_shape=(pltpu.VMEM((2,...]
    dot_general x7 -> x0, matrix products: 43.2 us -> none  [the longest x1 17.6 us: local(): jnp.einsum('mrk,mck->mrc', basis, right, precision=lax.Precision.HIGHEST)]
    all_gather x1 -> x0, waiting for transfers between devices: 39 us -> none  [local(): lax.all_gather(q_init.astype(jnp.bfloat16), 'tensor', axis=1, tiled=True)]
    another operation x12 -> x0, other arithmetic: 22 us -> none  [the longest x7 12 us: by_cholesky(): cholesky_factor = jnp.linalg.cholesky(gram_sum)]
    convert_element_type x2 -> x0, other arithmetic: 10.9 us -> none  [the longest x1 9.48 us: local(): (grads[0].astype(jnp.float32) + error[0].astype(jnp.float32)).astype(jnp....]
  transfers between devices with their start and end apart: 3 -> 0, of which waited for: 3 -> 0; matrix products, arithmetic and copies ran while one was open for 1% -> 0% of each run, Pallas kernels for 0% -> 0%
where the time goes in v2:
time: 79 us; the launch traced here: 78.9 us
  Pallas kernels  78.1 us (99%)
  between operations  0.8 us (1%)
    pallas_call x1, Pallas kernels, local(): pl.pallas_call(factors_kernel, name='factors', out_shape=(pltpu.VMEM((2,...  74.6 us
    pallas_call x1, Pallas kernels, local(): pl.pallas_call(store_kernel, name='store', out_shape=(pltpu.HBM((1, 2, 25...  3.48 us

profile of v2, /device:TPU:1, one launch (start us, length us, event | category | flops | bytes accessed | tf_op | source)
XLA Modules:
  0.0 78.9 jit_solution(10391739968181258084)
XLA Ops:
  0.6 74.6 %factors.1 = (bf16[2,256,8192]{2,1,0:T(8,128)(2,1)S(1)}, f32[2,32,256]{2,1,0:T(8,128)S(1)}, f32[2,32,256]{2,1,0:T(8,128)S(1)}) custom-call(bf16[1,2,256,8192]{3,2,1,0:T(8,128)(2,1)} %grads.1, bf16[1,2,256,8192]{3,2,1,0:T(8,128)(2,1)} %error.1, f32[2,32,256]{2,1,0:T(8,128)} %bitcast.3), custom_call_target="tpu_custom_call" | custom-call | tf_op jit(solution)/shard_map/factors/pallas_call | solution.py:309
  75.2 3.5 %store.1 = (bf16[1,2,256,8192]{3,2,1,0:T(8,128)(2,1)}, f32[2,32,256]{2,1,0:T(8,128)}, f32[2,32,256]{2,1,0:T(8,128)}) custom-call(bf16[2,256,8192]{2,1,0:T(8,128)(2,1)S(1)} %get-tuple-element.9.rest, f32[2,32,256]{2,1,0:T(8,128)S(1)} %get-tuple-element.10.p_in, f32[2,32,256]{2,1,0:T(8,128)S(1)} %get-tuple-element.11.q_in), custom_call_target="tpu_custom_call" | custom-call | tf_op jit(solution)/shard_map/store/pallas_call | solution.py:350

commit v3 on v2

--- a/solution.py
+++ b/solution.py
@@ -205,6 +205,8 @@
                 for k, (dx, dy) in enumerate(FAR_FIRST):
                     send(gram_in.at[sweep, chip], gram_in.at[sweep, chip], g_send.at[sweep, k], g_recv.at[sweep], plane(dx, dy))
 
+        sent = started[:]
+        started.clear()
         for h in range(2):
             landed(plane_in.at[sweep, h, pl.ds(0, 15)], rs_recv.at[sweep, h])
             total = plane_in[sweep, h, 0].astype(F32)
@@ -227,8 +229,8 @@
             basis_stage[...] = nn(inverse, left_sum[other], precision=HIGHEST)
             send(basis_stage, basis.at[core], basis_sem.at[0], basis_sem.at[1], sibling)
             basis[core] = nn(inverse, left_sum[core], precision=HIGHEST)
-        sent = started[:]
-        started.clear()
+        for copy in sent:
+            copy.wait_send()
         after = right_in.at[sweep + 1] if sweep < ITERS - 1 else right_last.at[core]
         for h in range(2):
             landed(z_in.at[sweep, h, pl.ds(0, 3)], z_recv.at[sweep, h])
@@ -237,8 +239,6 @@
                 total += z_in[sweep, h, k].astype(F32)
             after[h, chip] = (nn(inverse, total, precision=HIGHEST) * 0.25).astype(BF)
             gather(sweep + 1, h, after)
-        for copy in sent:
-            copy.wait_send()
 
     landed(basis.at[other], basis_sem.at[1])
     factor = []

time: 79 us -> 78.7 us (level)
  no operation moved by 1% of the time
where the time goes in v3:
time: 78.7 us; the launch traced here: 78.6 us
  Pallas kernels  77.8 us (99%)
  between operations  0.8 us (1%)
    pallas_call x1, Pallas kernels, local(): pl.pallas_call(factors_kernel, name='factors', out_shape=(pltpu.VMEM((2,...  74.3 us
    pallas_call x1, Pallas kernels, local(): pl.pallas_call(store_kernel, name='store', out_shape=(pltpu.HBM((1, 2, 25...  3.48 us

profile of v3, /device:TPU:1, one launch (start us, length us, event | category | flops | bytes accessed | tf_op | source)
XLA Modules:
  0.0 78.6 jit_solution(18367895983093769820)
XLA Ops:
  0.6 74.3 %factors.1 = (bf16[2,256,8192]{2,1,0:T(8,128)(2,1)S(1)}, f32[2,32,256]{2,1,0:T(8,128)S(1)}, f32[2,32,256]{2,1,0:T(8,128)S(1)}) custom-call(bf16[1,2,256,8192]{3,2,1,0:T(8,128)(2,1)} %grads.1, bf16[1,2,256,8192]{3,2,1,0:T(8,128)(2,1)} %error.1, f32[2,32,256]{2,1,0:T(8,128)} %bitcast.3), custom_call_target="tpu_custom_call" | custom-call | tf_op jit(solution)/shard_map/factors/pallas_call | solution.py:309
  75.0 3.5 %store.1 = (bf16[1,2,256,8192]{3,2,1,0:T(8,128)(2,1)}, f32[2,32,256]{2,1,0:T(8,128)}, f32[2,32,256]{2,1,0:T(8,128)}) custom-call(bf16[2,256,8192]{2,1,0:T(8,128)(2,1)S(1)} %get-tuple-element.9.rest, f32[2,32,256]{2,1,0:T(8,128)S(1)} %get-tuple-element.10.p_in, f32[2,32,256]{2,1,0:T(8,128)S(1)} %get-tuple-element.11.q_in), custom_call_target="tpu_custom_call" | custom-call | tf_op jit(solution)/shard_map/store/pallas_call | solution.py:350
